TPU v7x, 1024 devices: a whole 4x4x32 slice. The times are simulated.
1024 devices in a mesh: row: 8 (over x, core), col: 8 (over z_lo), grp: 16 (over y, z_hi).
Axes of the slice: x: 4, y: 4, z: 32 (z_hi: 4, z_lo: 8; z = z_hi * 8 + z_lo), core: 2. Of those that a mesh axis runs over, the one named last changes fastest.
Arguments:
- amplitudes: bfloat16 [512, 16, 1024], P(None, 'row', ('col', 'grp')), may hold values from -6 to 6
- ladder_integrals: bfloat16 [16, 1024, 64, 1024], P('row', None, 'grp', 'col'), may hold values from -0.046875 to 0.046875
- cycle_integrals: bfloat16 [16, 64, 16, 64], replicated, may hold values from -0.1875 to 0.1875
- pair_list: int32 [512, 2], replicated, may hold values from 0 to 127, as said below
- occ_energy: float32 [128], replicated, may hold values from -3 to -0.5
- batch_energy: float32 [64], replicated, may hold values from 0.2 to 4
- virt_energy: float32 [1024], P('col'), may hold values from 0.2 to 4
Outputs:
- update: float32 [16, 64, 32, 1024], P('row', None, 'grp', 'col')
Inputs may be any that keep to these rules, and one draw needn't show every extreme that they name: `pair_list`: pair p holds the occupied orbital of window row p // 32 and that of window column p % 32; the 16 row orbitals and 32 column orbitals are all distinct.
All inputs are finite; a program needn't handle non-finite values.
Results may differ from a plain program's by a relative error of at most 0.0029.
Values may be sent and summed in bfloat16 or wider, within the bound.
A program may use at most 32 MiB of HBM per device.

v0:
```python
import jax
import jax.numpy as jnp
from jax import lax
from jax.sharding import PartitionSpec as P

OCC_I = 16
OCC_J = 32


def local(
    amplitudes, ladder_integrals, cycle_integrals, pair_list, occ_energy, batch_energy, virt_energy
):
    cont_here, virt_all, batch_here, virt_here = ladder_integrals.shape
    occ_rows = OCC_I // lax.axis_size("row")
    occ_cols = OCC_J // lax.axis_size("grp")
    row_index = lax.axis_index("row")
    grp_index = lax.axis_index("grp")
    flat_ladder = ladder_integrals.reshape(cont_here, virt_all, batch_here * virt_here)
    partial_value = jnp.einsum(
        "pcd,cdx->px",
        lax.all_gather(amplitudes, ("col", "grp"), axis=2, tiled=True),
        flat_ladder,
        preferred_element_type=jnp.float32,
    )
    summed = lax.psum_scatter(partial_value, "row", scatter_dimension=0, tiled=True)
    ladder_part = summed.astype(jnp.bfloat16).reshape(occ_rows, OCC_J, batch_here, virt_here)
    regrouped = lax.all_to_all(ladder_part, "grp", split_axis=1, concat_axis=2, tiled=True)
    row_block = lax.dynamic_slice_in_dim(cycle_integrals, row_index * occ_rows, occ_rows, 0)
    cycle = jnp.einsum(
        "iakc,kjcb->iajb",
        row_block,
        lax.all_gather(regrouped, "row", axis=0, tiled=True),
        preferred_element_type=jnp.float32,
    )
    ladder_term = jnp.transpose(regrouped, (0, 2, 1, 3)).astype(jnp.float32)
    pair_grid = pair_list.reshape(OCC_I, OCC_J, 2)
    mine = lax.dynamic_slice_in_dim(pair_grid, row_index * occ_rows, occ_rows, 0)
    mine = lax.dynamic_slice_in_dim(mine, grp_index * occ_cols, occ_cols, 1)
    orbital_ids = lax.broadcasted_iota(jnp.int32, (1, 1, 1, occ_energy.shape[0]), 3)
    looked = jnp.sum(jnp.where(mine[:, :, :, None] == orbital_ids, occ_energy, 0.0), axis=-1)
    pair_energy = looked[:, :, 0] + looked[:, :, 1]
    denom = (
        pair_energy[:, None, :, None]
        - batch_energy[None, :, None, None]
        - virt_energy[None, None, None, :]
    )
    return (ladder_term + cycle) / denom


def solution(mesh):
    placed = (
        P(None, "row", ("col", "grp")),
        P("row", None, "grp", "col"),
        P(),
        P(),
        P(),
        P(),
        P("col"),
    )
    return jax.shard_map(
        local, mesh=mesh, in_specs=placed, out_specs=P("row", None, "grp", "col"), check_vma=False
    )
```

profile of v0, /device:TPU:1, one launch (start us, length us, event | category | flops | bytes accessed | tf_op | source)
XLA Modules:
  0.0 1237.6 jit_solution(7385586042936163252)
XLA Ops:
  6.5 0.0 all-gather.2.cloned.1.call-start
  6.5 0.7 all-gather.2.cloned.1.call-update
  7.3 0.0 reduce-scatter.2.cloned.1.call-start
  7.3 2.7 reshape.28
  10.1 0.0 copy-start
  10.1 0.0 copy-start.1
  10.1 953.8 %all-gather.2.cloned.1.call-done = bf16[512,2,1024]{0,2,1:T(8,128)(2,1)} async-done(((bf16[512,2,8]{0,2,1:T(8,128)(2,1)}), bf16[512,2,1024]{0,2,1:T(8,128)(2,1)}) %all-gather.2.cloned.1.call-update) | async-done | bytes 2097168 | tf_op jit(solution)/shard_map/all_gather | solution.py:21
  963.9 3.9 convolution_bitcast_fusion
  967.8 0.0 copy-start.2
  967.8 0.0 copy-start.3
  967.8 0.0 reduce-scatter.2.cloned.1.call-update
  967.8 0.0 copy-done
  967.8 0.1 reshape.30
  967.9 0.1 constant_dynamic-slice_fusion
  968.0 0.1 copy.32
  968.1 0.0 copy-done.1
  968.1 0.2 fusion.3
  968.2 196.3 %reduce-scatter.2.cloned.1.call-done = f32[64,512]{1,0:T(8,128)} async-done(((f32[512,512]{1,0:T(8,128)}), f32[64,512]{1,0:T(8,128)}) %reduce-scatter.2.cloned.1.call-update) | async-done | bytes 131088 | tf_op jit(solution)/shard_map/reduce_scatter | solution.py:25
  1164.5 0.9 convert_element_type.9
  1165.5 0.7 copy.28
  1166.1 22.4 %all-to-all-start = ((bf16[2,32,4,128]{3,2,0,1:T(4,128)(2,1)}), bf16[2,32,4,128]{3,2,0,1:T(4,128)(2,1)S(1)}, u32[]{:S(2)}, u32[]{:S(2)}) async-start(bf16[2,32,4,128]{3,2,0,1:T(4,128)(2,1)} %copy.28), calls=%async_computation.1 | async-start | bytes 131072 | tf_op jit(solution)/shard_map/all_to_all | solution.py:27
  1188.6 0.1 slice_add_fusion
  1188.6 0.1 copy.38
  1188.7 1.1 constant_dynamic-slice_fusion.1
  1189.8 0.0 copy-done.2
  1189.8 0.1 broadcast_subtract_fusion
  1189.9 22.1 %all-to-all-done = bf16[2,32,4,128]{3,2,0,1:T(4,128)(2,1)S(1)} async-done(((bf16[2,32,4,128]{3,2,0,1:T(4,128)(2,1)}), bf16[2,32,4,128]{3,2,0,1:T(4,128)(2,1)S(1)}, u32[]{:S(2)}, u32[]{:S(2)}) %all-to-all-start) | async-done | bytes 65568 | tf_op jit(solution)/shard_map/all_to_all | solution.py:27
  1212.0 17.6 %all_gather.7 = bf16[16,2,64,128]{3,2,0,1:T(8,128)(2,1)S(1)} all-gather(bf16[2,2,64,128]{3,2,0,1:T(8,128)(2,1)S(1)} %bitcast.27), channel_id=1, replica_groups=mesh['row'=8,'col'=8,'grp'=16] {'row'}, dimensions={0}, use_global_device_ids=true | all-gather | bytes 589824 | tf_op jit(solution)/shard_map/all_gather | solution.py:32
  1229.7 0.0 copy-done.3
  1229.7 0.3 fusion.1
  1230.0 0.8 copy.34
  (2 shorter events, 0.0 us)
Async XLA Ops:
  6.5 957.4 %all-gather.2.cloned.1.call-start = ((), (), s32[]{:S(2)}) async-start(), calls=%async_computation.2 | async-start | bytes 2113536 | tf_op jit(solution)/shard_map/all_gather | solution.py:21
  7.3 1157.3 %reduce-scatter.2.cloned.1.call-start = ((), (), s32[]{:S(2)}) async-start(), calls=%async_computation.3 | async-start | bytes 1179648 | tf_op jit(solution)/shard_map/reduce_scatter | solution.py:25
  10.1 957.8 %copy-start = (s32[512,2]{0,1:T(2,128)S(1)}, s32[512,2]{0,1:T(2,128)}, u32[]{:S(2)}) copy-start(s32[512,2]{0,1:T(2,128)} %param.10) | copy-start | bytes 12292
  10.1 958.0 %copy-start.1 = (f32[128]{0:T(128)S(1)}, f32[128]{0:T(128)}, u32[]{:S(2)}) copy-start(f32[128]{0:T(128)} %param.11) | copy-start | bytes 1540
  967.8 222.0 %copy-start.2 = (f32[64]{0:T(128)S(1)}, f32[64]{0:T(128)}, u32[]{:S(2)}) copy-start(f32[64]{0:T(128)} %param.12) | copy-start | bytes 772
  967.8 261.9 %copy-start.3 = (f32[128]{0:T(128)S(1)}, f32[128]{0:T(128)}, u32[]{:S(2)}) copy-start(f32[128]{0:T(128)} %param.13) | copy-start | bytes 1540
  1166.1 45.9 %all-to-all-start = ((bf16[2,32,4,128]{3,2,0,1:T(4,128)(2,1)}), bf16[2,32,4,128]{3,2,0,1:T(4,128)(2,1)S(1)}, u32[]{:S(2)}, u32[]{:S(2)}) async-start(bf16[2,32,4,128]{3,2,0,1:T(4,128)(2,1)} %copy.28), calls=%async_computation.1 | async-start | bytes 131072 | tf_op jit(solution)/shard_map/all_to_all | solution.py:27
Sparse Core Ops, SparseCore 0:
  10.0 953.8 all-gather.1
  967.9 196.5 reduce-scatter.1
where the time goes:
time: 1240 us
  waiting for transfers between devices  1170 us (94%)
  starting transfers between devices  22.5 us (2%)
  blocking collectives  17.6 us (1%)
  between operations  13.5 us (1%)
    all_gather x1, waiting for transfers between devices, local(): lax.all_gather(amplitudes, ('col', 'grp'), axis=2, tiled=True)  954 us
    reduce_scatter x1, waiting for transfers between devices, local(): lax.psum_scatter(partial_value, 'row', scatter_dimension=0, tiled=True)  196 us
  transfers between devices with their start and end apart: 3, of which 3 were waited for; matrix products, arithmetic and copies ran while one was open for 0% of the time, Pallas kernels for 0%

commit v1 on v0

v1 whole, which is shorter than its diff:
```python
import jax
import jax.numpy as jnp
from jax import lax
from jax.experimental import pallas as pl
from jax.experimental.pallas import tpu as pltpu
from jax.sharding import PartitionSpec as P

MESH = pl.DeviceIdType.MESH
F32 = jnp.float32
BF16 = jnp.bfloat16
NX, NY, NZ = 4, 4, 32
ROUNDS = 8


def dot(a, b, contract=((1,), (0,))):
    return lax.dot_general(a, b, (contract, ((), ())), preferred_element_type=F32)


def wrap(value, n):
    return lax.rem(value + 2 * n, n)


def kernel(
    amp_hbm, ladder_hbm, cycle_hbm, pair_ref, occ_ref, batch_ref, virt_ref, out_ref,
    buf, vraw, vwide, vmat, acc, sib, xsend, xrecv, ctmp, csend, crecv, dbuf,
    kraw, kwide, kmat, den,
    in_sem, zp_send, zp_recv, zm_send, zm_recv, yp_send, yp_recv, ym_send, ym_recv,
    hp_send, hp_recv, hm_send, hm_recv, s_send, s_recv, x_send, x_recv,
    c_send, c_recv, d_send, d_recv, e_send, e_recv,
):
    row = lax.axis_index("row")
    col = lax.axis_index("col")
    grp = lax.axis_index("grp")
    x, core = row // 2, lax.rem(row, 2)
    y = grp // 4
    z = lax.rem(grp, 4) * 8 + col

    def at(dx=0, dy=0, dz=0, flip=False):
        nx, ny, nz = wrap(x + dx, NX), wrap(y + dy, NY), wrap(z + dz, NZ)
        return (nx * 2 + (1 - core if flip else core), lax.rem(nz, 8), ny * 4 + nz // 8)

    def remote(src, dst, send, recv, device):
        return pltpu.make_async_remote_copy(
            src_ref=src, dst_ref=dst, send_sem=send, recv_sem=recv,
            device_id=device, device_id_type=MESH,
        )

    right, left = at(dz=1), at(dz=-1)
    up, down = at(dy=1), at(dy=-1)
    twin = at(flip=True)

    own_copy = pltpu.make_async_copy(amp_hbm, buf.at[0, 0], in_sem.at[0])
    v_copy = pltpu.make_async_copy(ladder_hbm, vraw, in_sem.at[1])
    k_copy = pltpu.make_async_copy(
        cycle_hbm.at[pl.ds(pl.multiple_of(row * 2048, 2048), 2048), :], kraw, in_sem.at[2]
    )
    own_copy.start()
    v_copy.start()
    k_copy.start()

    barrier = pltpu.get_barrier_semaphore()
    near = [right, left, up, down, twin, at(dx=1), at(dx=2), at(dx=3)]
    for device in near:
        pl.semaphore_signal(barrier, inc=1, device_id=device, device_id_type=MESH)
    pl.semaphore_wait(barrier, len(near))

    def z_plus(m, src):
        return remote(src, buf.at[0, 2 * m + 1], zp_send.at[m], zp_recv.at[m], right)

    def z_minus(m, src):
        return remote(src, buf.at[0, 2 * m + 2], zm_send.at[m], zm_recv.at[m], left)

    def four(slot, q):
        return buf.at[slot, pl.ds(4 * q, 4)]

    def y_plus(q):
        return remote(four(0, q), four(1, q), yp_send.at[q], yp_recv.at[q], up)

    def y_minus(q):
        return remote(four(0, q), four(2, q), ym_send.at[q], ym_recv.at[q], down)

    def half_plus(q):
        return remote(
            buf.at[1, pl.ds(4 * q, 2)], buf.at[3, pl.ds(4 * q, 2)],
            hp_send.at[q], hp_recv.at[q], up,
        )

    def half_minus(q):
        return remote(
            buf.at[2, pl.ds(4 * q + 2, 2)], buf.at[3, pl.ds(4 * q + 2, 2)],
            hm_send.at[q], hm_recv.at[q], down,
        )

    z_plus(0, amp_hbm).start()
    z_minus(0, amp_hbm).start()
    acc[...] = jnp.zeros_like(acc)
    own_copy.wait()
    v_copy.wait()

    def relayout(q):
        for slot, dy in enumerate((0, -1, 1, 2)):
            for e in range(4):
                dz = (2 * q, -2 * q - 1, 2 * q + 1, -2 * q - 2)[e]
                ny, nz = wrap(y + dy, NY), wrap(z + dz, NZ)
                shard = lax.rem(nz, 8) * 16 + ny * 4 + nz // 8
                for c in range(2):
                    start = pl.multiple_of(c * 4096 + shard * 32, 32)
                    to = ((slot * 4 + e) * 2 + c) * 32
                    vwide[pl.ds(to, 32), :] = vraw[pl.ds(start, 32), :].astype(F32)
        for a in range(4):
            vmat[q, :, pl.ds(a * 128, 128)] = vwide[pl.ds(a, 256, stride=4), :].astype(BF16)

    def multiply(q, block):
        lanes = pl.ds(pl.multiple_of(block * 128, 128), 128)
        lhs = buf[:, pl.ds(4 * q, 4), :, lanes].reshape(256, 128)
        product = dot(lhs, vmat[q], ((0,), (0,)))
        acc[0, block] += product[:, :256]
        acc[1, block] += product[:, 256:]

    @pl.loop(0, ROUNDS + 1)
    def _(q):
        @pl.when(q < ROUNDS)
        def _():
            for m in (2 * q, 2 * q + 1):
                z_plus(m, amp_hbm).wait_recv()

                @pl.when(m < 15)
                def _():
                    z_plus(m + 1, buf.at[0, 2 * m + 1]).start()
                    z_minus(m, amp_hbm).wait_recv()

                @pl.when(m < 14)
                def _():
                    z_minus(m + 1, buf.at[0, 2 * m + 2]).start()

            y_plus(q).start()
            y_minus(q).start()

        @pl.when(q > 0)
        def _():
            y_plus(q - 1).wait_recv()
            half_plus(q - 1).start()
            y_minus(q - 1).wait_recv()
            half_minus(q - 1).start()

        @pl.when(q < ROUNDS)
        def _():
            relayout(q)

        @pl.when(q > 1)
        def _():
            half_plus(q - 2).wait_recv()
            half_minus(q - 2).wait_recv()

            @pl.loop(0, 4)
            def _(block):
                multiply(q - 2, block)

    last = ROUNDS - 1
    half_plus(last).wait_recv()
    half_minus(last).wait_recv()

    def s_copy(dx):
        block = wrap(x + dx, NX)
        return remote(acc.at[1 - core, block], sib.at[block], s_send.at[dx], s_recv.at[dx], twin)

    def x_copy(dx):
        return remote(
            xsend.at[dx - 1], xrecv.at[dx - 1], x_send.at[dx - 1], x_recv.at[dx - 1], at(dx=dx)
        )

    for dx in (2, 1, 3, 0):
        multiply(last, wrap(x + dx, NX))
        s_copy(dx).start()
    for dx in (2, 1, 3):
        block = wrap(x + dx, NX)
        s_copy(dx).wait_recv()
        xsend[dx - 1] = acc[core, block] + sib[block]
        x_copy(dx).start()

    k_copy.wait()
    kwide[...] = kraw[...].astype(F32)
    from_c = lax.broadcasted_iota(jnp.int32, (64, 256), 0)
    lane = lax.broadcasted_iota(jnp.int32, (64, 256), 1)
    lane_c = (lane % 128) // 8 * 4 + lane // 128 * 2 + lane % 2
    places = [
        jnp.where((lane_c == from_c) & (lane % 8 // 2 == i), 1.0, 0.0).astype(BF16)
        for i in range(4)
    ]
    for nx in range(4):
        total = jnp.zeros((128, 256), F32)
        for i in range(4):
            part = kwide[pl.ds(nx * 4 + i, 128, stride=16), :].astype(BF16)
            total = total + dot(part, places[i])
        kmat[nx * 2] = total[:, :128].astype(BF16)
        kmat[nx * 2 + 1] = total[:, 128:].astype(BF16)

    s_copy(0).wait_recv()
    ladder = acc[core, x] + sib[x]
    for dx in (1, 3, 2):
        x_copy(dx).wait_recv()
        ladder = ladder + xrecv[dx - 1]

    for i in range(4):
        for a in range(2):
            ctmp[pl.ds(i * 2 + a, 32, stride=8), :] = ladder[
                i * 32:(i + 1) * 32, a * 128:(a + 1) * 128
            ]
    csend[...] = ctmp[...].astype(BF16).reshape(16, 16, 128)

    def c_copy(d):
        other = lax.rem(grp + d, 16)
        return remote(
            csend.at[other], crecv.at[grp], c_send.at[d], c_recv.at[d], (row, col, other)
        )

    order = (2, 6, 10, 14, 1, 3, 5, 7, 9, 11, 13, 15, 4, 8, 12)
    for d in order:
        c_copy(d).start()
    crecv[grp] = csend[grp]

    def column(ref, n):
        wide = jnp.broadcast_to(ref[...], (n, n))
        diagonal = lax.broadcasted_iota(jnp.int32, (n, n), 0) == lax.broadcasted_iota(
            jnp.int32, (n, n), 1
        )
        return jnp.sum(jnp.where(diagonal, wide, 0.0), axis=1, keepdims=True)

    occ = column(occ_ref, 128)
    orbital = lax.broadcasted_iota(jnp.int32, (128, 512), 0)
    first = jnp.sum(jnp.where(pair_ref[0:1, :] == orbital, occ, 0.0), axis=0, keepdims=True)
    second = jnp.sum(jnp.where(pair_ref[1:2, :] == orbital, occ, 0.0), axis=0, keepdims=True)
    energy = first + second
    pair = lax.broadcasted_iota(jnp.int32, (1, 512), 1)
    batch = column(batch_ref, 64)
    for i in range(2):
        for j in range(2):
            mine = (row * 2 + i) * 32 + grp * 2 + j
            one = jnp.sum(jnp.where(pair == mine, energy, 0.0), axis=1, keepdims=True)
            den[i, j] = one - batch - virt_ref[...]

    for d in order:
        c_copy(d).wait_recv()
    blocks = crecv[...].astype(F32).reshape(16, 2, 8, 128)
    for j in range(2):
        dbuf[x, core, :, pl.ds(j * 128, 128)] = blocks[:, j].reshape(128, 128).astype(BF16)

    def d_copy(dx):
        return remote(
            dbuf.at[x, core], dbuf.at[x, core], d_send.at[dx - 1], d_recv.at[dx - 1], at(dx=dx)
        )

    def e_copy(dx):
        block = dbuf.at[wrap(x - dx, NX), core]
        return remote(block, block, e_send.at[dx], e_recv.at[dx], twin)

    for dx in (2, 1, 3):
        d_copy(dx).start()
    e_copy(0).start()

    out_row = lax.broadcasted_iota(jnp.int32, (128, 128), 0)
    lane = lax.broadcasted_iota(jnp.int32, (128, 128), 1)
    same = (out_row % 64 // 4 == lane // 8) & (out_row % 2 == lane % 2)
    same = same & (core * 2 + out_row // 64 == lane % 8 // 2)

    def pick(part):
        return jnp.where(same & (out_row % 4 // 2 == part), 1.0, 0.0).astype(BF16)

    def term(dx, part):
        block = wrap(x - dx, NX)
        return dot(kmat[block * 2 + part], dbuf[block, part])

    total = term(0, core) + dot(pick(core), dbuf[x, core])
    for dx in (1, 3, 2):
        d_copy(dx).wait_recv()
        e_copy(dx).start()
        total = total + term(dx, core)
    e_copy(0).wait_recv()
    total = total + term(0, 1 - core) + dot(pick(1 - core), dbuf[x, 1 - core])
    for dx in (1, 3, 2):
        e_copy(dx).wait_recv()
        total = total + term(dx, 1 - core)
    for i in range(2):
        for j in range(2):
            value = total[i * 64:(i + 1) * 64, j * 128:(j + 1) * 128] / den[i, j]
            out_ref[pl.ds(i * 128 + j, 64, stride=2), :] = value

    @pl.loop(0, 16)
    def _(m):
        z_plus(m, buf.at[0, 0]).wait_send()

        @pl.when(m < 15)
        def _():
            z_minus(m, buf.at[0, 0]).wait_send()

    @pl.loop(0, ROUNDS)
    def _(q):
        y_plus(q).wait_send()
        y_minus(q).wait_send()
        half_plus(q).wait_send()
        half_minus(q).wait_send()

    for dx in range(4):
        s_copy(dx).wait_send()
        e_copy(dx).wait_send()
        if dx:
            x_copy(dx).wait_send()
            d_copy(dx).wait_send()
    for d in order:
        c_copy(d).wait_send()


def local(
    amplitudes, ladder_integrals, cycle_integrals, pair_list, occ_energy, batch_energy, virt_energy
):
    any_spec = pl.BlockSpec(memory_space=pl.ANY)
    vmem = pl.BlockSpec(memory_space=pltpu.VMEM)
    dma = pltpu.SemaphoreType.DMA
    counts = (3, 16, 16, 15, 15, 8, 8, 8, 8, 8, 8, 8, 8, 4, 4, 3, 3, 16, 16, 3, 3, 4, 4)
    out = pl.pallas_call(
        kernel,
        out_shape=jax.ShapeDtypeStruct((256, 128), F32),
        in_specs=[any_spec] * 3 + [vmem] * 4,
        out_specs=vmem,
        scratch_shapes=[
            pltpu.VMEM((4, 32, 16, 512), BF16),
            pltpu.VMEM((8192, 128), BF16),
            pltpu.VMEM((1024, 128), F32),
            pltpu.VMEM((8, 256, 512), BF16),
            pltpu.VMEM((2, 4, 128, 256), F32),
            pltpu.VMEM((4, 128, 256), F32),
            pltpu.VMEM((3, 128, 256), F32),
            pltpu.VMEM((3, 128, 256), F32),
            pltpu.VMEM((256, 128), F32),
            pltpu.VMEM((16, 16, 128), BF16),
            pltpu.VMEM((16, 16, 128), BF16),
            pltpu.VMEM((4, 2, 128, 256), BF16),
            pltpu.VMEM((2048, 64), BF16),
            pltpu.VMEM((2048, 64), F32),
            pltpu.VMEM((8, 128, 128), BF16),
            pltpu.VMEM((2, 2, 64, 128), F32),
        ] + [dma((n,)) for n in counts],
        compiler_params=pltpu.CompilerParams(
            collective_id=0, has_side_effects=True, vmem_limit_bytes=48 * 1024 * 1024
        ),
    )(
        jnp.transpose(amplitudes, (1, 2, 0)).reshape(16, 512),
        ladder_integrals.reshape(8192, 128),
        cycle_integrals.reshape(16384, 64),
        jnp.transpose(pair_list),
        occ_energy.reshape(1, 128),
        batch_energy.reshape(1, 64),
        virt_energy.reshape(1, 128),
    )
    return out.reshape(2, 64, 2, 128)


def solution(mesh):
    placed = (
        P(None, "row", ("col", "grp")),
        P("row", None, "grp", "col"),
        P(),
        P(),
        P(),
        P(),
        P("col"),
    )
    return jax.shard_map(
        local, mesh=mesh, in_specs=placed, out_specs=P("row", None, "grp", "col"), check_vma=False
    )
```

time: 1240 us -> 112 us (0.09)
  waiting for transfers between devices: 1170 us -> 0 us
  Pallas kernels: 0 us -> 107 us
  starting transfers between devices: 22.5 us -> 0 us
  blocking collectives: 17.6 us -> 0 us
  between operations: 13.5 us -> 0.02 us
    all_gather x1 -> x0, waiting for transfers between devices: 954 us -> none  [local(): lax.all_gather(amplitudes, ('col', 'grp'), axis=2, tiled=True)]
    reduce_scatter x1 -> x0, waiting for transfers between devices: 196 us -> none  [local(): lax.psum_scatter(partial_value, 'row', scatter_dimension=0, tiled=True)]
    pallas_call x0 -> x1, Pallas kernels: none -> 107 us  [local(): pl.pallas_call(kernel, out_shape=jax.ShapeDtypeStruct((256, 128), F32), i...]
    all_to_all x1 -> x0, starting transfers between devices: 22.4 us -> none  [local(): lax.all_to_all(ladder_part, 'grp', split_axis=1, concat_axis=2, tiled=True)]
    all_to_all x1 -> x0, waiting for transfers between devices: 22.1 us -> none  [local(): lax.all_to_all(ladder_part, 'grp', split_axis=1, concat_axis=2, tiled=True)]
    all_gather x1 -> x0, blocking collectives: 17.6 us -> none  [local(): lax.all_gather(regrouped, 'row', axis=0, tiled=True)]
  transfers between devices with their start and end apart: 3 -> 0, of which waited for: 3 -> 0; matrix products, arithmetic and copies ran while one was open for 0% -> 0% of each run, Pallas kernels for 0% -> 0%
where the time goes in v1:
time: 112 us
  Pallas kernels  107 us (96%)
  local copies, waits for them, and re-layouts  5.62 us (5%)
    pallas_call x1, Pallas kernels, local(): pl.pallas_call(kernel, out_shape=jax.ShapeDtypeStruct((256, 128), F32), i...  107 us
    unnamed x13, local copies, waits for them, and re-layouts  5.62 us

profile of v1, /device:TPU:1, one launch (start us, length us, event | category | flops | bytes accessed | tf_op | source)
XLA Modules:
  0.0 112.2 jit_solution(9209535534807347130)
XLA Ops:
  0.0 0.0 copy-start
  0.0 1.6 %copy-done = bf16[2,1024,4,128]{3,2,1,0:T(4,128)(2,1)S(1)} copy-done((bf16[2,1024,4,128]{3,2,1,0:T(4,128)(2,1)S(1)}, bf16[2,1024,4,128]{3,2,1,0:T(4,128)(2,1)}, u32[]{:S(2)}) %copy-start) | copy-done | bytes 2097176
  1.6 0.0 copy-start.1
  1.6 0.7 copy-done.1
  2.3 0.0 copy-start.2
  2.3 0.7 copy-done.2
  3.0 0.0 copy-start.3
  3.0 0.7 copy-done.3
  3.7 0.0 copy-start.4
  3.7 0.7 copy-done.4
  4.3 0.0 copy-start.5
  4.3 0.7 copy-done.5
  5.0 106.6 %shard_map.73 = f32[256,128]{1,0:T(8,128)S(1)} custom-call(bf16[16,512]{1,0:T(8,128)(2,1)S(1)} %bitcast.12, bf16[8192,128]{1,0:T(8,128)(2,1)S(1)} %bitcast.10, bf16[16384,64]{1,0:T(8,128)(2,1)} %bitcast.17, s32[2,512]{1,0:T(2,128)S(1)} %bitcast.13, f32[1,128]{1,0:T(1,128)S(1)} %bitcast.14, f32[1,64]{1,0:T(1,128)S(1)} %bitcast.15, f32[1,128]{1,0:T(1,128)S(1)} %bitcast.16), custom_call_target="tpu_custom_call" | custom-call | tf_op jit(solution)/shard_map/pallas_call | solution.py:320
  111.5 0.7 copy.9
Async XLA Ops:
  0.0 1.6 %copy-start = (bf16[2,1024,4,128]{3,2,1,0:T(4,128)(2,1)S(1)}, bf16[2,1024,4,128]{3,2,1,0:T(4,128)(2,1)}, u32[]{:S(2)}) copy-start(bf16[2,1024,4,128]{3,2,1,0:T(4,128)(2,1)} %param.8) | copy-start | bytes 6291460
  1.6 0.7 copy-start.1
  2.3 0.7 copy-start.2
  3.0 0.7 copy-start.3
  3.7 0.7 copy-start.4
  4.3 0.7 copy-start.5

commit v2 on v1

--- a/solution.py
+++ b/solution.py
@@ -21,10 +21,10 @@
 
 
 def kernel(
-    amp_hbm, ladder_hbm, cycle_hbm, pair_ref, occ_ref, batch_ref, virt_ref, out_ref,
-    buf, vraw, vwide, vmat, acc, sib, xsend, xrecv, ctmp, csend, crecv, dbuf,
+    amp_hbm, ladder_hbm, cycle_hbm, pair_hbm, occ_hbm, batch_hbm, virt_hbm, out_ref,
+    pair_ref, occ_ref, batch_ref, virt_ref, buf, vraw, vwide, vmat, acc, sib, xsend, xrecv, ctmp, csend, crecv, dbuf,
     kraw, kwide, kmat, den,
-    in_sem, zp_send, zp_recv, zm_send, zm_recv, yp_send, yp_recv, ym_send, ym_recv,
+    in_sem, z_send, z_recv, yp_send, yp_recv, ym_send, ym_recv,
     hp_send, hp_recv, hm_send, hm_recv, s_send, s_recv, x_send, x_recv,
     c_send, c_recv, d_send, d_recv, e_send, e_recv,
 ):
@@ -45,7 +45,6 @@
             device_id=device, device_id_type=MESH,
         )
 
-    right, left = at(dz=1), at(dz=-1)
     up, down = at(dy=1), at(dy=-1)
     twin = at(flip=True)
 
@@ -54,21 +53,45 @@
     k_copy = pltpu.make_async_copy(
         cycle_hbm.at[pl.ds(pl.multiple_of(row * 2048, 2048), 2048), :], kraw, in_sem.at[2]
     )
+    small = [
+        pltpu.make_async_copy(src, dst, in_sem.at[3 + i])
+        for i, (src, dst) in enumerate(
+            ((pair_hbm, pair_ref), (occ_hbm, occ_ref), (batch_hbm, batch_ref), (virt_hbm, virt_ref))
+        )
+    ]
     own_copy.start()
     v_copy.start()
     k_copy.start()
+    for copy in small:
+        copy.start()
 
     barrier = pltpu.get_barrier_semaphore()
-    near = [right, left, up, down, twin, at(dx=1), at(dx=2), at(dx=3)]
+    near = [at(dz=d) for d in (1, -1, 2, -2, 3, -3, 4, -4)]
+    near += [up, down, twin, at(dx=1), at(dx=2), at(dx=3)]
     for device in near:
         pl.semaphore_signal(barrier, inc=1, device_id=device, device_id_type=MESH)
     pl.semaphore_wait(barrier, len(near))
 
-    def z_plus(m, src):
-        return remote(src, buf.at[0, 2 * m + 1], zp_send.at[m], zp_recv.at[m], right)
-
-    def z_minus(m, src):
-        return remote(src, buf.at[0, 2 * m + 2], zm_send.at[m], zm_recv.at[m], left)
+    def place(t):
+        return 2 * t - 1 if t > 0 else -2 * t
+
+    def z_copy(t):
+        sign, far = (1, t) if t > 0 else (-1, -t)
+        step = far % 4 or 4
+        source = amp_hbm if far == step else buf.at[0, place(sign * (far - step))]
+        return remote(
+            source, buf.at[0, place(t)], z_send.at[place(t)], z_recv.at[place(t)], at(dz=sign * step)
+        )
+
+    def pass_on(*heads):
+        for more in (4, 1, 2, 3):
+            for sign, far in heads:
+                if sign * (far + more) != -16:
+                    z_copy(sign * (far + more)).start()
+
+    def arrived(*shards):
+        for t in shards:
+            z_copy(t).wait_recv()
 
     def four(slot, q):
         return buf.at[slot, pl.ds(4 * q, 4)]
@@ -91,8 +114,7 @@
             hm_send.at[q], hm_recv.at[q], down,
         )
 
-    z_plus(0, amp_hbm).start()
-    z_minus(0, amp_hbm).start()
+    pass_on((1, 0), (-1, 0))
     acc[...] = jnp.zeros_like(acc)
     own_copy.wait()
     v_copy.wait()
@@ -117,48 +139,67 @@
         acc[0, block] += product[:, :256]
         acc[1, block] += product[:, 256:]
 
-    @pl.loop(0, ROUNDS + 1)
+    @pl.loop(0, ROUNDS)
     def _(q):
-        @pl.when(q < ROUNDS)
-        def _():
-            for m in (2 * q, 2 * q + 1):
-                z_plus(m, amp_hbm).wait_recv()
-
-                @pl.when(m < 15)
-                def _():
-                    z_plus(m + 1, buf.at[0, 2 * m + 1]).start()
-                    z_minus(m, amp_hbm).wait_recv()
-
-                @pl.when(m < 14)
-                def _():
-                    z_minus(m + 1, buf.at[0, 2 * m + 2]).start()
-
-            y_plus(q).start()
-            y_minus(q).start()
-
-        @pl.when(q > 0)
-        def _():
-            y_plus(q - 1).wait_recv()
-            half_plus(q - 1).start()
-            y_minus(q - 1).wait_recv()
-            half_minus(q - 1).start()
-
-        @pl.when(q < ROUNDS)
-        def _():
-            relayout(q)
-
-        @pl.when(q > 1)
-        def _():
-            half_plus(q - 2).wait_recv()
-            half_minus(q - 2).wait_recv()
-
-            @pl.loop(0, 4)
-            def _(block):
-                multiply(q - 2, block)
+        relayout(q)
+
+    def y_start(q):
+        y_plus(q).start()
+        y_minus(q).start()
+
+    def y_next(q):
+        y_plus(q).wait_recv()
+        half_plus(q).start()
+        y_minus(q).wait_recv()
+        half_minus(q).start()
+
+    def y_done(q):
+        half_plus(q).wait_recv()
+        half_minus(q).wait_recv()
+
+    def products(q):
+        y_done(q)
+
+        @pl.loop(0, 4)
+        def _(block):
+            multiply(q, block)
 
     last = ROUNDS - 1
-    half_plus(last).wait_recv()
-    half_minus(last).wait_recv()
+    arrived(1, -1, 2)
+    y_start(0)
+    arrived(-2, 3, -3, 4, -4)
+    pass_on((1, 4), (-1, 4))
+    y_start(1)
+    y_next(0)
+    arrived(5, -5, 6)
+    y_start(2)
+    y_next(1)
+    arrived(-6, 7, -7, 8, -8)
+    pass_on((1, 8), (-1, 8))
+    y_start(3)
+    products(0)
+    y_next(2)
+    products(1)
+    arrived(9, -9, 10)
+    y_start(4)
+    y_next(3)
+    arrived(-10, 11, -11, 12, -12)
+    pass_on((1, 12), (-1, 12))
+    y_start(5)
+    products(2)
+    products(3)
+    y_next(4)
+    arrived(13, -13, 14)
+    y_start(6)
+    y_next(5)
+    arrived(-14, 15, -15, 16)
+    y_start(7)
+    products(4)
+    products(5)
+    y_next(6)
+    y_next(7)
+    products(6)
+    y_done(last)
 
     def s_copy(dx):
         block = wrap(x + dx, NX)
@@ -219,6 +260,8 @@
         c_copy(d).start()
     crecv[grp] = csend[grp]
 
+    for copy in small:
+        copy.wait()
     def column(ref, n):
         wide = jnp.broadcast_to(ref[...], (n, n))
         diagonal = lax.broadcasted_iota(jnp.int32, (n, n), 0) == lax.broadcasted_iota(
@@ -285,13 +328,9 @@
             value = total[i * 64:(i + 1) * 64, j * 128:(j + 1) * 128] / den[i, j]
             out_ref[pl.ds(i * 128 + j, 64, stride=2), :] = value
 
-    @pl.loop(0, 16)
-    def _(m):
-        z_plus(m, buf.at[0, 0]).wait_send()
-
-        @pl.when(m < 15)
-        def _():
-            z_minus(m, buf.at[0, 0]).wait_send()
+    for t in range(-15, 17):
+        if t:
+            z_copy(t).wait_send()
 
     @pl.loop(0, ROUNDS)
     def _(q):
@@ -313,16 +352,19 @@
 def local(
     amplitudes, ladder_integrals, cycle_integrals, pair_list, occ_energy, batch_energy, virt_energy
 ):
-    any_spec = pl.BlockSpec(memory_space=pl.ANY)
-    vmem = pl.BlockSpec(memory_space=pltpu.VMEM)
+    hbm = pl.BlockSpec(memory_space=pltpu.HBM)
     dma = pltpu.SemaphoreType.DMA
-    counts = (3, 16, 16, 15, 15, 8, 8, 8, 8, 8, 8, 8, 8, 4, 4, 3, 3, 16, 16, 3, 3, 4, 4)
+    counts = (7, 32, 32, 8, 8, 8, 8, 8, 8, 8, 8, 4, 4, 3, 3, 16, 16, 3, 3, 4, 4)
     out = pl.pallas_call(
         kernel,
         out_shape=jax.ShapeDtypeStruct((256, 128), F32),
-        in_specs=[any_spec] * 3 + [vmem] * 4,
-        out_specs=vmem,
+        in_specs=[hbm] * 7,
+        out_specs=pl.BlockSpec(memory_space=pltpu.VMEM),
         scratch_shapes=[
+            pltpu.VMEM((2, 512), jnp.int32),
+            pltpu.VMEM((1, 128), F32),
+            pltpu.VMEM((1, 64), F32),
+            pltpu.VMEM((1, 128), F32),
             pltpu.VMEM((4, 32, 16, 512), BF16),
             pltpu.VMEM((8192, 128), BF16),
             pltpu.VMEM((1024, 128), F32),

time: 112 us -> 94.9 us (0.85); the launches traced: 112 us -> 93.6 us
  Pallas kernels: 107 us -> 87.9 us
    pallas_call x1, Pallas kernels: 107 us -> 87.9 us  [local(): pl.pallas_call(kernel, out_shape=jax.ShapeDtypeStruct((256, 128), F32), i...]
where the time goes in v2:
time: 94.9 us; the launch traced here: 93.6 us
  Pallas kernels  87.9 us (93%)
  local copies, waits for them, and re-layouts  5.62 us (6%)
    pallas_call x1, Pallas kernels, local(): pl.pallas_call(kernel, out_shape=jax.ShapeDtypeStruct((256, 128), F32), i...  87.9 us
    unnamed x13, local copies, waits for them, and re-layouts  5.62 us

profile of v2, /device:TPU:1, one launch (start us, length us, event | category | flops | bytes accessed | tf_op | source)
XLA Modules:
  0.0 93.6 jit_solution(1481547836091068347)
XLA Ops:
  0.0 0.0 copy-start
  0.0 1.6 %copy-done = bf16[2,1024,4,128]{3,2,1,0:T(4,128)(2,1)S(1)} copy-done((bf16[2,1024,4,128]{3,2,1,0:T(4,128)(2,1)S(1)}, bf16[2,1024,4,128]{3,2,1,0:T(4,128)(2,1)}, u32[]{:S(2)}) %copy-start) | copy-done | bytes 2097176
  1.6 0.0 copy-start.1
  1.6 0.7 copy-done.1
  2.3 0.0 copy-start.2
  2.3 0.7 copy-done.2
  3.0 0.0 copy-start.3
  3.0 0.7 copy-done.3
  3.7 0.0 copy-start.4
  3.7 0.7 copy-done.4
  4.3 0.0 copy-start.5
  4.3 0.7 copy-done.5
  5.0 87.9 %shard_map.73 = f32[256,128]{1,0:T(8,128)S(1)} custom-call(bf16[16,512]{1,0:T(8,128)(2,1)S(1)} %bitcast.12, bf16[8192,128]{1,0:T(8,128)(2,1)S(1)} %bitcast.10, bf16[16384,64]{1,0:T(8,128)(2,1)} %bitcast.17, s32[2,512]{1,0:T(2,128)S(1)} %bitcast.13, f32[1,128]{1,0:T(1,128)S(1)} %bitcast.14, f32[1,64]{1,0:T(1,128)S(1)} %bitcast.15, f32[1,128]{1,0:T(1,128)S(1)} %bitcast.16), custom_call_target="tpu_custom_call" | custom-call | tf_op jit(solution)/shard_map/pallas_call | solution.py:358
  92.9 0.7 copy.9
Async XLA Ops:
  0.0 1.6 %copy-start = (bf16[2,1024,4,128]{3,2,1,0:T(4,128)(2,1)S(1)}, bf16[2,1024,4,128]{3,2,1,0:T(4,128)(2,1)}, u32[]{:S(2)}) copy-start(bf16[2,1024,4,128]{3,2,1,0:T(4,128)(2,1)} %param.8) | copy-start | bytes 6291460
  1.6 0.7 copy-start.1
  2.3 0.7 copy-start.2
  3.0 0.7 copy-start.3
  3.7 0.7 copy-start.4
  4.3 0.7 copy-start.5

commit v3 on v2

--- a/solution.py
+++ b/solution.py
@@ -10,6 +10,7 @@
 BF16 = jnp.bfloat16
 NX, NY, NZ = 4, 4, 32
 ROUNDS = 8
+DIRECT = 6
 
 
 def dot(a, b, contract=((1,), (0,))):
@@ -22,8 +23,8 @@
 
 def kernel(
     amp_hbm, ladder_hbm, cycle_hbm, pair_hbm, occ_hbm, batch_hbm, virt_hbm, out_ref,
-    pair_ref, occ_ref, batch_ref, virt_ref, buf, vraw, vwide, vmat, acc, sib, xsend, xrecv, ctmp, csend, crecv, dbuf,
-    kraw, kwide, kmat, den,
+    pair_ref, occ_ref, batch_ref, virt_ref, buf, vraw, vwide, vmat, acc, sib, xsend, xrecv, xfar, ctmp, csend, crecv, dnear, dfar,
+    kraw, kwide, kmat, kfar, den,
     in_sem, z_send, z_recv, yp_send, yp_recv, ym_send, ym_recv,
     hp_send, hp_recv, hm_send, hm_recv, s_send, s_recv, x_send, x_recv,
     c_send, c_recv, d_send, d_recv, e_send, e_recv,
@@ -67,7 +68,7 @@
 
     barrier = pltpu.get_barrier_semaphore()
     near = [at(dz=d) for d in (1, -1, 2, -2, 3, -3, 4, -4)]
-    near += [up, down, twin, at(dx=1), at(dx=2), at(dx=3)]
+    near += [at(dy=2), up, down, twin, at(dx=1), at(dx=2), at(dx=3)]
     for device in near:
         pl.semaphore_signal(barrier, inc=1, device_id=device, device_id_type=MESH)
     pl.semaphore_wait(barrier, len(near))
@@ -113,6 +114,9 @@
             buf.at[2, pl.ds(4 * q + 2, 2)], buf.at[3, pl.ds(4 * q + 2, 2)],
             hm_send.at[q], hm_recv.at[q], down,
         )
+
+    def y_two(q):
+        return remote(four(0, q), four(3, q), hp_send.at[q], hp_recv.at[q], at(dy=2))
 
     pass_on((1, 0), (-1, 0))
     acc[...] = jnp.zeros_like(acc)
@@ -144,16 +148,23 @@
         relayout(q)
 
     def y_start(q):
+        if q >= DIRECT:
+            y_two(q).start()
         y_plus(q).start()
         y_minus(q).start()
 
     def y_next(q):
         y_plus(q).wait_recv()
-        half_plus(q).start()
+        if q < DIRECT:
+            half_plus(q).start()
         y_minus(q).wait_recv()
-        half_minus(q).start()
+        if q < DIRECT:
+            half_minus(q).start()
 
     def y_done(q):
+        if q >= DIRECT:
+            y_two(q).wait_recv()
+            return
         half_plus(q).wait_recv()
         half_minus(q).wait_recv()
 
@@ -206,9 +217,8 @@
         return remote(acc.at[1 - core, block], sib.at[block], s_send.at[dx], s_recv.at[dx], twin)
 
     def x_copy(dx):
-        return remote(
-            xsend.at[dx - 1], xrecv.at[dx - 1], x_send.at[dx - 1], x_recv.at[dx - 1], at(dx=dx)
-        )
+        src, dst = (xfar.at[0], xfar.at[1]) if dx == 2 else (xsend.at[dx // 2], xrecv.at[dx // 2])
+        return remote(src, dst, x_send.at[dx - 1], x_recv.at[dx - 1], at(dx=dx))
 
     for dx in (2, 1, 3, 0):
         multiply(last, wrap(x + dx, NX))
@@ -216,31 +226,40 @@
     for dx in (2, 1, 3):
         block = wrap(x + dx, NX)
         s_copy(dx).wait_recv()
-        xsend[dx - 1] = acc[core, block] + sib[block]
+        both = acc[core, block] + sib[block]
+        if dx == 2:
+            xfar[0] = both.astype(BF16)
+        else:
+            xsend[dx // 2] = both
         x_copy(dx).start()
 
     k_copy.wait()
     kwide[...] = kraw[...].astype(F32)
     from_c = lax.broadcasted_iota(jnp.int32, (64, 256), 0)
     lane = lax.broadcasted_iota(jnp.int32, (64, 256), 1)
-    lane_c = (lane % 128) // 8 * 4 + lane // 128 * 2 + lane % 2
-    places = [
-        jnp.where((lane_c == from_c) & (lane % 8 // 2 == i), 1.0, 0.0).astype(BF16)
-        for i in range(4)
-    ]
+    y_part = lane % 32 // 8 * 16 + lane % 2
+    step_part = lane % 128 // 32
+    from_zh = lax.rem(grp + jnp.where(step_part == 2, 3, step_part), 4)
+    near_c = y_part + from_zh * 4 + lane // 128 * 2
+    far_c = y_part + lax.rem(grp + 2, 4) * 4 + lane // 32 % 2 * 2
+    far_total = jnp.zeros((128, 256), F32)
     for nx in range(4):
         total = jnp.zeros((128, 256), F32)
         for i in range(4):
             part = kwide[pl.ds(nx * 4 + i, 128, stride=16), :].astype(BF16)
-            total = total + dot(part, places[i])
+            mine = lane % 8 // 2 == i
+            total = total + dot(part, jnp.where(mine & (near_c == from_c), 1.0, 0.0).astype(BF16))
+            mine = mine & (lane // 64 == nx) & (far_c == from_c)
+            far_total = far_total + dot(part, jnp.where(mine, 1.0, 0.0).astype(BF16))
         kmat[nx * 2] = total[:, :128].astype(BF16)
         kmat[nx * 2 + 1] = total[:, 128:].astype(BF16)
+    kfar[...] = far_total.astype(BF16)
 
     s_copy(0).wait_recv()
     ladder = acc[core, x] + sib[x]
     for dx in (1, 3, 2):
         x_copy(dx).wait_recv()
-        ladder = ladder + xrecv[dx - 1]
+        ladder = ladder + (xfar[1].astype(F32) if dx == 2 else xrecv[dx // 2])
 
     for i in range(4):
         for a in range(2):
@@ -282,47 +301,70 @@
             one = jnp.sum(jnp.where(pair == mine, energy, 0.0), axis=1, keepdims=True)
             den[i, j] = one - batch - virt_ref[...]
 
-    for d in order:
-        c_copy(d).wait_recv()
-    blocks = crecv[...].astype(F32).reshape(16, 2, 8, 128)
-    for j in range(2):
-        dbuf[x, core, :, pl.ds(j * 128, 128)] = blocks[:, j].reshape(128, 128).astype(BF16)
-
-    def d_copy(dx):
-        return remote(
-            dbuf.at[x, core], dbuf.at[x, core], d_send.at[dx - 1], d_recv.at[dx - 1], at(dx=dx)
-        )
-
-    def e_copy(dx):
-        block = dbuf.at[wrap(x - dx, NX), core]
-        return remote(block, block, e_send.at[dx], e_recv.at[dx], twin)
-
-    for dx in (2, 1, 3):
-        d_copy(dx).start()
-    e_copy(0).start()
-
-    out_row = lax.broadcasted_iota(jnp.int32, (128, 128), 0)
-    lane = lax.broadcasted_iota(jnp.int32, (128, 128), 1)
-    same = (out_row % 64 // 4 == lane // 8) & (out_row % 2 == lane % 2)
-    same = same & (core * 2 + out_row // 64 == lane % 8 // 2)
-
-    def pick(part):
-        return jnp.where(same & (out_row % 4 // 2 == part), 1.0, 0.0).astype(BF16)
-
-    def term(dx, part):
-        block = wrap(x - dx, NX)
-        return dot(kmat[block * 2 + part], dbuf[block, part])
-
-    total = term(0, core) + dot(pick(core), dbuf[x, core])
-    for dx in (1, 3, 2):
-        d_copy(dx).wait_recv()
-        e_copy(dx).start()
-        total = total + term(dx, core)
-    e_copy(0).wait_recv()
-    total = total + term(0, 1 - core) + dot(pick(1 - core), dbuf[x, 1 - core])
-    for dx in (1, 3, 2):
-        e_copy(dx).wait_recv()
-        total = total + term(dx, 1 - core)
+    def block(step):
+        from_zh = lax.rem(grp + step, 4)
+        four_y = jnp.stack([crecv[i * 4 + from_zh] for i in range(4)])
+        halves = four_y.astype(F32).reshape(4, 2, 8, 128)
+        return [halves[:, j].reshape(32, 128).astype(BF16) for j in range(2)]
+
+    def d_copy(dx, part):
+        one = (dfar if part else dnear).at[x, core]
+        sem = part * 3 + dx - 1
+        return remote(one, one, d_send.at[sem], d_recv.at[sem], at(dx=dx))
+
+    def e_copy(dx, part):
+        one = (dfar if part else dnear).at[wrap(x - dx, NX), core]
+        sem = part * 4 + dx
+        return remote(one, one, e_send.at[sem], e_recv.at[sem], twin)
+
+    for part in range(2):
+        for d in reversed(order):
+            if (d % 4 == 2) == (part == 1):
+                c_copy(d).wait_recv()
+        for place_here, step in enumerate((2,) if part else (0, 1, 3)):
+            for j, half in enumerate(block(step)):
+                to = dfar if part else dnear
+                to[x, core, pl.ds(place_here * 32, 32), pl.ds(j * 128, 128)] = half
+        for dx in (2, 1, 3):
+            d_copy(dx, part).start()
+        e_copy(0, part).start()
+    for part in range(2):
+        for dx in (1, 3, 2):
+            d_copy(dx, part).wait_recv()
+            e_copy(dx, part).start()
+
+    def select(width, own_lane, zh_lane, core_lane):
+        out_row = lax.broadcasted_iota(jnp.int32, (128, width), 0)
+        lane = lax.broadcasted_iota(jnp.int32, (128, width), 1)
+        same = (out_row % 64 // 16 == lane % 32 // 8) & (out_row % 2 == lane % 2)
+        same = same & (core * 2 + out_row // 64 == lane % 8 // 2)
+        same = same & (out_row % 16 // 4 == zh_lane(lane)) & own_lane(lane)
+        same = same & (out_row % 4 // 2 == core_lane(lane))
+        return jnp.where(same, 1.0, 0.0).astype(BF16)
+
+    def near_zh(lane):
+        return lax.rem(grp + jnp.where(lane // 32 == 2, 3, lane // 32), 4)
+
+    picks = [
+        select(128, lambda lane: lane < 96, near_zh, lambda lane: jnp.full_like(lane, c))
+        for c in range(2)
+    ]
+    far_pick = select(
+        256, lambda lane: lane // 64 == x, lambda lane: jnp.full_like(lane, lax.rem(grp + 2, 4)),
+        lambda lane: lane // 32 % 2,
+    )
+    for dx in range(4):
+        e_copy(dx, 0).wait_recv()
+    total = jnp.zeros((128, 256), F32)
+    for nx in range(4):
+        for c in range(2):
+            total = total + dot(kmat[nx * 2 + c, :, :96], dnear[nx, c])
+    for c in range(2):
+        total = total + dot(picks[c][:, :96], dnear[x, c])
+    for dx in range(4):
+        e_copy(dx, 1).wait_recv()
+    far = dfar[...].reshape(256, 256)
+    total = total + dot(kfar[...], far) + dot(far_pick, far)
     for i in range(2):
         for j in range(2):
             value = total[i * 64:(i + 1) * 64, j * 128:(j + 1) * 128] / den[i, j]
@@ -336,15 +378,24 @@
     def _(q):
         y_plus(q).wait_send()
         y_minus(q).wait_send()
-        half_plus(q).wait_send()
-        half_minus(q).wait_send()
+
+        @pl.when(q < DIRECT)
+        def _():
+            half_plus(q).wait_send()
+            half_minus(q).wait_send()
+
+        @pl.when(q >= DIRECT)
+        def _():
+            y_two(q).wait_send()
 
     for dx in range(4):
         s_copy(dx).wait_send()
-        e_copy(dx).wait_send()
+        e_copy(dx, 0).wait_send()
+        e_copy(dx, 1).wait_send()
         if dx:
             x_copy(dx).wait_send()
-            d_copy(dx).wait_send()
+            d_copy(dx, 0).wait_send()
+            d_copy(dx, 1).wait_send()
     for d in order:
         c_copy(d).wait_send()
 
@@ -354,10 +405,10 @@
 ):
     hbm = pl.BlockSpec(memory_space=pltpu.HBM)
     dma = pltpu.SemaphoreType.DMA
-    counts = (7, 32, 32, 8, 8, 8, 8, 8, 8, 8, 8, 4, 4, 3, 3, 16, 16, 3, 3, 4, 4)
+    counts = (7, 32, 32, 8, 8, 8, 8, 8, 8, 8, 8, 4, 4, 3, 3, 16, 16, 6, 6, 8, 8)
     out = pl.pallas_call(
         kernel,
-        out_shape=jax.ShapeDtypeStruct((256, 128), F32),
+        out_shape=pltpu.VMEM((256, 128), F32),
         in_specs=[hbm] * 7,
         out_specs=pl.BlockSpec(memory_space=pltpu.VMEM),
         scratch_shapes=[
@@ -371,19 +422,22 @@
             pltpu.VMEM((8, 256, 512), BF16),
             pltpu.VMEM((2, 4, 128, 256), F32),
             pltpu.VMEM((4, 128, 256), F32),
-            pltpu.VMEM((3, 128, 256), F32),
-            pltpu.VMEM((3, 128, 256), F32),
+            pltpu.VMEM((2, 128, 256), F32),
+            pltpu.VMEM((2, 128, 256), F32),
+            pltpu.VMEM((2, 128, 256), BF16),
             pltpu.VMEM((256, 128), F32),
             pltpu.VMEM((16, 16, 128), BF16),
             pltpu.VMEM((16, 16, 128), BF16),
-            pltpu.VMEM((4, 2, 128, 256), BF16),
+            pltpu.VMEM((4, 2, 96, 256), BF16),
+            pltpu.VMEM((4, 2, 32, 256), BF16),
             pltpu.VMEM((2048, 64), BF16),
             pltpu.VMEM((2048, 64), F32),
             pltpu.VMEM((8, 128, 128), BF16),
+            pltpu.VMEM((128, 256), BF16),
             pltpu.VMEM((2, 2, 64, 128), F32),
         ] + [dma((n,)) for n in counts],
         compiler_params=pltpu.CompilerParams(
-            collective_id=0, has_side_effects=True, vmem_limit_bytes=48 * 1024 * 1024
+            collective_id=0, has_side_effects=True, vmem_limit_bytes=60 * 1024 * 1024
         ),
     )(
         jnp.transpose(amplitudes, (1, 2, 0)).reshape(16, 512),

time: 94.9 us -> 85.8 us (0.904); the launches traced: 93.6 us -> 85.7 us
  local copies, waits for them, and re-layouts: 5.62 us -> 0.66 us
  Pallas kernels: 87.9 us -> 85 us
    unnamed x13 -> x1, local copies, waits for them, and re-layouts: 5.62 us -> 0.66 us
    pallas_call x1, Pallas kernels: 87.9 us -> 85 us  [local(): pl.pallas_call(kernel, out_shape=pltpu.VMEM((256, 128), F32), in_specs=[h...]
where the time goes in v3:
time: 85.8 us; the launch traced here: 85.7 us
  Pallas kernels  85 us (99%)
    pallas_call x1, Pallas kernels, local(): pl.pallas_call(kernel, out_shape=pltpu.VMEM((256, 128), F32), in_specs=[h...  85 us

profile of v3, /device:TPU:1, one launch (start us, length us, event | category | flops | bytes accessed | tf_op | source)
XLA Modules:
  0.0 85.7 jit_solution(13817794868376743417)
XLA Ops:
  0.0 85.0 %shard_map.73 = f32[256,128]{1,0:T(8,128)S(1)} custom-call(bf16[16,512]{1,0:T(8,128)(2,1)} %bitcast.13, bf16[8192,128]{1,0:T(8,128)(2,1)} %bitcast.12, bf16[16384,64]{1,0:T(8,128)(2,1)} %bitcast.11, s32[2,512]{1,0:T(2,128)} %bitcast.14, f32[1,128]{1,0:T(1,128)} %bitcast.15, f32[1,64]{1,0:T(1,128)} %bitcast.16, f32[1,128]{1,0:T(1,128)} %bitcast.17), custom_call_target="tpu_custom_call" | custom-call | tf_op jit(solution)/shard_map/pallas_call | solution.py:409
  85.0 0.7 copy.9

commit v4 on v3

--- a/solution.py
+++ b/solution.py
@@ -10,7 +10,7 @@
 BF16 = jnp.bfloat16
 NX, NY, NZ = 4, 4, 32
 ROUNDS = 8
-DIRECT = 6
+DIRECT = 3
 
 
 def dot(a, b, contract=((1,), (0,))):
@@ -23,7 +23,7 @@
 
 def kernel(
     amp_hbm, ladder_hbm, cycle_hbm, pair_hbm, occ_hbm, batch_hbm, virt_hbm, out_ref,
-    pair_ref, occ_ref, batch_ref, virt_ref, buf, vraw, vwide, vmat, acc, sib, xsend, xrecv, xfar, ctmp, csend, crecv, dnear, dfar,
+    pair_ref, occ_ref, batch_ref, virt_ref, buf, vraw, vwide, vmat, acc, sib, xsend, xrecv, ctmp, csend, crecv, dnear, dfar,
     kraw, kwide, kmat, kfar, den,
     in_sem, z_send, z_recv, yp_send, yp_recv, ym_send, ym_recv,
     hp_send, hp_recv, hm_send, hm_recv, s_send, s_recv, x_send, x_recv,
@@ -60,17 +60,13 @@
             ((pair_hbm, pair_ref), (occ_hbm, occ_ref), (batch_hbm, batch_ref), (virt_hbm, virt_ref))
         )
     ]
+    barrier = pltpu.get_barrier_semaphore()
+    near = [at(dz=d) for d in (4, -4, 3, -3, 2, -2, 1, -1)]
+    near += [at(dy=2), up, down, at(dx=2), at(dx=1), at(dx=3), twin]
+    for device in near:
+        pl.semaphore_signal(barrier, inc=1, device_id=device, device_id_type=MESH)
     own_copy.start()
     v_copy.start()
-    k_copy.start()
-    for copy in small:
-        copy.start()
-
-    barrier = pltpu.get_barrier_semaphore()
-    near = [at(dz=d) for d in (1, -1, 2, -2, 3, -3, 4, -4)]
-    near += [at(dy=2), up, down, twin, at(dx=1), at(dx=2), at(dx=3)]
-    for device in near:
-        pl.semaphore_signal(barrier, inc=1, device_id=device, device_id_type=MESH)
     pl.semaphore_wait(barrier, len(near))
 
     def place(t):
@@ -94,15 +90,6 @@
         for t in shards:
             z_copy(t).wait_recv()
 
-    def four(slot, q):
-        return buf.at[slot, pl.ds(4 * q, 4)]
-
-    def y_plus(q):
-        return remote(four(0, q), four(1, q), yp_send.at[q], yp_recv.at[q], up)
-
-    def y_minus(q):
-        return remote(four(0, q), four(2, q), ym_send.at[q], ym_recv.at[q], down)
-
     def half_plus(q):
         return remote(
             buf.at[1, pl.ds(4 * q, 2)], buf.at[3, pl.ds(4 * q, 2)],
@@ -115,10 +102,22 @@
             hm_send.at[q], hm_recv.at[q], down,
         )
 
+    def rows(q):
+        return pl.ds(4 * q, 4) if q < 7 else pl.ds(2 * q + 14, 2)
+
     def y_two(q):
-        return remote(four(0, q), four(3, q), hp_send.at[q], hp_recv.at[q], at(dy=2))
+        return remote(buf.at[0, rows(q)], buf.at[3, rows(q)], hp_send.at[q], hp_recv.at[q], at(dy=2))
+
+    def y_plus(q):
+        return remote(buf.at[0, rows(q)], buf.at[1, rows(q)], yp_send.at[q], yp_recv.at[q], up)
+
+    def y_minus(q):
+        return remote(buf.at[0, rows(q)], buf.at[2, rows(q)], ym_send.at[q], ym_recv.at[q], down)
 
     pass_on((1, 0), (-1, 0))
+    k_copy.start()
+    for copy in small:
+        copy.start()
     acc[...] = jnp.zeros_like(acc)
     own_copy.wait()
     v_copy.wait()
@@ -203,22 +202,24 @@
     arrived(13, -13, 14)
     y_start(6)
     y_next(5)
-    arrived(-14, 15, -15, 16)
+    arrived(-14, 15)
     y_start(7)
+    arrived(-15, 16)
+    y_start(8)
     products(4)
     products(5)
     y_next(6)
-    y_next(7)
     products(6)
-    y_done(last)
+    for pair in (7, 8):
+        y_next(pair)
+        y_done(pair)
 
     def s_copy(dx):
         block = wrap(x + dx, NX)
         return remote(acc.at[1 - core, block], sib.at[block], s_send.at[dx], s_recv.at[dx], twin)
 
     def x_copy(dx):
-        src, dst = (xfar.at[0], xfar.at[1]) if dx == 2 else (xsend.at[dx // 2], xrecv.at[dx // 2])
-        return remote(src, dst, x_send.at[dx - 1], x_recv.at[dx - 1], at(dx=dx))
+        return remote(xsend.at[dx - 1], xrecv.at[dx - 1], x_send.at[dx - 1], x_recv.at[dx - 1], at(dx=dx))
 
     for dx in (2, 1, 3, 0):
         multiply(last, wrap(x + dx, NX))
@@ -226,11 +227,7 @@
     for dx in (2, 1, 3):
         block = wrap(x + dx, NX)
         s_copy(dx).wait_recv()
-        both = acc[core, block] + sib[block]
-        if dx == 2:
-            xfar[0] = both.astype(BF16)
-        else:
-            xsend[dx // 2] = both
+        xsend[dx - 1] = (acc[core, block] + sib[block]).astype(BF16)
         x_copy(dx).start()
 
     k_copy.wait()
@@ -259,7 +256,7 @@
     ladder = acc[core, x] + sib[x]
     for dx in (1, 3, 2):
         x_copy(dx).wait_recv()
-        ladder = ladder + (xfar[1].astype(F32) if dx == 2 else xrecv[dx // 2])
+        ladder = ladder + xrecv[dx - 1].astype(F32)
 
     for i in range(4):
         for a in range(2):
@@ -301,6 +298,24 @@
             one = jnp.sum(jnp.where(pair == mine, energy, 0.0), axis=1, keepdims=True)
             den[i, j] = one - batch - virt_ref[...]
 
+    for t in range(-15, 17):
+        if t:
+            z_copy(t).wait_send()
+
+    for q in range(ROUNDS + 1):
+        y_plus(q).wait_send()
+        y_minus(q).wait_send()
+        if q < DIRECT:
+            half_plus(q).wait_send()
+            half_minus(q).wait_send()
+        else:
+            y_two(q).wait_send()
+
+    for dx in range(4):
+        s_copy(dx).wait_send()
+        if dx:
+            x_copy(dx).wait_send()
+
     def block(step):
         from_zh = lax.rem(grp + step, 4)
         four_y = jnp.stack([crecv[i * 4 + from_zh] for i in range(4)])
@@ -328,10 +343,8 @@
         for dx in (2, 1, 3):
             d_copy(dx, part).start()
         e_copy(0, part).start()
-    for part in range(2):
-        for dx in (1, 3, 2):
-            d_copy(dx, part).wait_recv()
-            e_copy(dx, part).start()
+    for d in order:
+        c_copy(d).wait_send()
 
     def select(width, own_lane, zh_lane, core_lane):
         out_row = lax.broadcasted_iota(jnp.int32, (128, width), 0)
@@ -353,6 +366,11 @@
         256, lambda lane: lane // 64 == x, lambda lane: jnp.full_like(lane, lax.rem(grp + 2, 4)),
         lambda lane: lane // 32 % 2,
     )
+    for part in range(2):
+        for dx in (1, 3, 2):
+            d_copy(dx, part).wait_recv()
+            e_copy(dx, part).start()
+
     for dx in range(4):
         e_copy(dx, 0).wait_recv()
     total = jnp.zeros((128, 256), F32)
@@ -370,34 +388,11 @@
             value = total[i * 64:(i + 1) * 64, j * 128:(j + 1) * 128] / den[i, j]
             out_ref[pl.ds(i * 128 + j, 64, stride=2), :] = value
 
-    for t in range(-15, 17):
-        if t:
-            z_copy(t).wait_send()
-
-    @pl.loop(0, ROUNDS)
-    def _(q):
-        y_plus(q).wait_send()
-        y_minus(q).wait_send()
-
-        @pl.when(q < DIRECT)
-        def _():
-            half_plus(q).wait_send()
-            half_minus(q).wait_send()
-
-        @pl.when(q >= DIRECT)
-        def _():
-            y_two(q).wait_send()
-
     for dx in range(4):
-        s_copy(dx).wait_send()
-        e_copy(dx, 0).wait_send()
-        e_copy(dx, 1).wait_send()
-        if dx:
-            x_copy(dx).wait_send()
-            d_copy(dx, 0).wait_send()
-            d_copy(dx, 1).wait_send()
-    for d in order:
-        c_copy(d).wait_send()
+        for part in range(2):
+            e_copy(dx, part).wait_send()
+            if dx:
+                d_copy(dx, part).wait_send()
 
 
 def local(
@@ -405,7 +400,7 @@
 ):
     hbm = pl.BlockSpec(memory_space=pltpu.HBM)
     dma = pltpu.SemaphoreType.DMA
-    counts = (7, 32, 32, 8, 8, 8, 8, 8, 8, 8, 8, 4, 4, 3, 3, 16, 16, 6, 6, 8, 8)
+    counts = (7, 32, 32, 9, 9, 9, 9, 9, 9, 9, 9, 4, 4, 3, 3, 16, 16, 6, 6, 8, 8)
     out = pl.pallas_call(
         kernel,
         out_shape=pltpu.VMEM((256, 128), F32),
@@ -422,9 +417,8 @@
             pltpu.VMEM((8, 256, 512), BF16),
             pltpu.VMEM((2, 4, 128, 256), F32),
             pltpu.VMEM((4, 128, 256), F32),
-            pltpu.VMEM((2, 128, 256), F32),
-            pltpu.VMEM((2, 128, 256), F32),
-            pltpu.VMEM((2, 128, 256), BF16),
+            pltpu.VMEM((3, 128, 256), BF16),
+            pltpu.VMEM((3, 128, 256), BF16),
             pltpu.VMEM((256, 128), F32),
             pltpu.VMEM((16, 16, 128), BF16),
             pltpu.VMEM((16, 16, 128), BF16),

time: 85.8 us -> 83.8 us (0.977)
  Pallas kernels: 85 us -> 83 us
    pallas_call x1, Pallas kernels: 85 us -> 83 us  [local(): pl.pallas_call(kernel, out_shape=pltpu.VMEM((256, 128), F32), in_specs=[h...]
where the time goes in v4:
time: 83.8 us; the launch traced here: 83.7 us
  Pallas kernels  83 us (99%)
    pallas_call x1, Pallas kernels, local(): pl.pallas_call(kernel, out_shape=pltpu.VMEM((256, 128), F32), in_specs=[h...  83 us

profile of v4, /device:TPU:1, one launch (start us, length us, event | category | flops | bytes accessed | tf_op | source)
XLA Modules:
  0.0 83.7 jit_solution(13345925331514437855)
XLA Ops:
  0.0 83.0 %shard_map.73 = f32[256,128]{1,0:T(8,128)S(1)} custom-call(bf16[16,512]{1,0:T(8,128)(2,1)} %bitcast.13, bf16[8192,128]{1,0:T(8,128)(2,1)} %bitcast.12, bf16[16384,64]{1,0:T(8,128)(2,1)} %bitcast.11, s32[2,512]{1,0:T(2,128)} %bitcast.14, f32[1,128]{1,0:T(1,128)} %bitcast.15, f32[1,64]{1,0:T(1,128)} %bitcast.16, f32[1,128]{1,0:T(1,128)} %bitcast.17), custom_call_target="tpu_custom_call" | custom-call | tf_op jit(solution)/shard_map/pallas_call | solution.py:404
  83.0 0.7 copy.9

commit v5 on v4

--- a/solution.py
+++ b/solution.py
@@ -10,7 +10,7 @@
 BF16 = jnp.bfloat16
 NX, NY, NZ = 4, 4, 32
 ROUNDS = 8
-DIRECT = 3
+DIRECT = 0
 
 
 def dot(a, b, contract=((1,), (0,))):
@@ -183,33 +183,28 @@
     y_next(0)
     arrived(5, -5, 6)
     y_start(2)
-    y_next(1)
     arrived(-6, 7, -7, 8, -8)
     pass_on((1, 8), (-1, 8))
     y_start(3)
+    y_next(1)
     products(0)
-    y_next(2)
-    products(1)
     arrived(9, -9, 10)
     y_start(4)
-    y_next(3)
     arrived(-10, 11, -11, 12, -12)
     pass_on((1, 12), (-1, 12))
     y_start(5)
-    products(2)
-    products(3)
-    y_next(4)
+    y_next(2)
+    products(1)
     arrived(13, -13, 14)
     y_start(6)
-    y_next(5)
     arrived(-14, 15)
     y_start(7)
     arrived(-15, 16)
     y_start(8)
-    products(4)
-    products(5)
-    y_next(6)
-    products(6)
+    products(2)
+    for q in range(3, 7):
+        y_next(q)
+        products(q)
     for pair in (7, 8):
         y_next(pair)
         y_done(pair)
@@ -229,6 +224,65 @@
         s_copy(dx).wait_recv()
         xsend[dx - 1] = (acc[core, block] + sib[block]).astype(BF16)
         x_copy(dx).start()
+
+    for t in range(-15, 17):
+        if t:
+            z_copy(t).wait_send()
+
+    for q in range(ROUNDS + 1):
+        y_plus(q).wait_send()
+        y_minus(q).wait_send()
+        if q < DIRECT:
+            half_plus(q).wait_send()
+            half_minus(q).wait_send()
+        else:
+            y_two(q).wait_send()
+
+    s_copy(0).wait_recv()
+    ladder = acc[core, x] + sib[x]
+    for dx in (1, 3, 2):
+        x_copy(dx).wait_recv()
+        ladder = ladder + xrecv[dx - 1].astype(F32)
+
+    for i in range(4):
+        for a in range(2):
+            ctmp[pl.ds(i * 2 + a, 32, stride=8), :] = ladder[
+                i * 32:(i + 1) * 32, a * 128:(a + 1) * 128
+            ]
+    csend[...] = ctmp[...].astype(BF16).reshape(16, 16, 128)
+
+    def c_copy(d):
+        other = lax.rem(grp + d, 16)
+        return remote(
+            csend.at[other], crecv.at[grp], c_send.at[d], c_recv.at[d], (row, col, other)
+        )
+
+    order = (2, 6, 10, 14, 1, 3, 5, 7, 9, 11, 13, 15, 4, 8, 12)
+    for d in order:
+        c_copy(d).start()
+    crecv[grp] = csend[grp]
+
+    for copy in small:
+        copy.wait()
+    def column(ref, n):
+        wide = jnp.broadcast_to(ref[...], (n, n))
+        diagonal = lax.broadcasted_iota(jnp.int32, (n, n), 0) == lax.broadcasted_iota(
+            jnp.int32, (n, n), 1
+        )
+        return jnp.sum(jnp.where(diagonal, wide, 0.0), axis=1, keepdims=True)
+
+    occ = column(occ_ref, 128)
+    orbital = lax.broadcasted_iota(jnp.int32, (128, 512), 0)
+    first = jnp.sum(jnp.where(pair_ref[0:1, :] == orbital, occ, 0.0), axis=0, keepdims=True)
+    second = jnp.sum(jnp.where(pair_ref[1:2, :] == orbital, occ, 0.0), axis=0, keepdims=True)
+    energy = first + second
+    pair = lax.broadcasted_iota(jnp.int32, (1, 512), 1)
+    batch = column(batch_ref, 64)
+    for i in range(2):
+        for j in range(2):
+            mine = (row * 2 + i) * 32 + grp * 2 + j
+            one = jnp.sum(jnp.where(pair == mine, energy, 0.0), axis=1, keepdims=True)
+            den[i, j] = one - batch - virt_ref[...]
 
     k_copy.wait()
     kwide[...] = kraw[...].astype(F32)
@@ -251,65 +305,6 @@
         kmat[nx * 2] = total[:, :128].astype(BF16)
         kmat[nx * 2 + 1] = total[:, 128:].astype(BF16)
     kfar[...] = far_total.astype(BF16)
-
-    s_copy(0).wait_recv()
-    ladder = acc[core, x] + sib[x]
-    for dx in (1, 3, 2):
-        x_copy(dx).wait_recv()
-        ladder = ladder + xrecv[dx - 1].astype(F32)
-
-    for i in range(4):
-        for a in range(2):
-            ctmp[pl.ds(i * 2 + a, 32, stride=8), :] = ladder[
-                i * 32:(i + 1) * 32, a * 128:(a + 1) * 128
-            ]
-    csend[...] = ctmp[...].astype(BF16).reshape(16, 16, 128)
-
-    def c_copy(d):
-        other = lax.rem(grp + d, 16)
-        return remote(
-            csend.at[other], crecv.at[grp], c_send.at[d], c_recv.at[d], (row, col, other)
-        )
-
-    order = (2, 6, 10, 14, 1, 3, 5, 7, 9, 11, 13, 15, 4, 8, 12)
-    for d in order:
-        c_copy(d).start()
-    crecv[grp] = csend[grp]
-
-    for copy in small:
-        copy.wait()
-    def column(ref, n):
-        wide = jnp.broadcast_to(ref[...], (n, n))
-        diagonal = lax.broadcasted_iota(jnp.int32, (n, n), 0) == lax.broadcasted_iota(
-            jnp.int32, (n, n), 1
-        )
-        return jnp.sum(jnp.where(diagonal, wide, 0.0), axis=1, keepdims=True)
-
-    occ = column(occ_ref, 128)
-    orbital = lax.broadcasted_iota(jnp.int32, (128, 512), 0)
-    first = jnp.sum(jnp.where(pair_ref[0:1, :] == orbital, occ, 0.0), axis=0, keepdims=True)
-    second = jnp.sum(jnp.where(pair_ref[1:2, :] == orbital, occ, 0.0), axis=0, keepdims=True)
-    energy = first + second
-    pair = lax.broadcasted_iota(jnp.int32, (1, 512), 1)
-    batch = column(batch_ref, 64)
-    for i in range(2):
-        for j in range(2):
-            mine = (row * 2 + i) * 32 + grp * 2 + j
-            one = jnp.sum(jnp.where(pair == mine, energy, 0.0), axis=1, keepdims=True)
-            den[i, j] = one - batch - virt_ref[...]
-
-    for t in range(-15, 17):
-        if t:
-            z_copy(t).wait_send()
-
-    for q in range(ROUNDS + 1):
-        y_plus(q).wait_send()
-        y_minus(q).wait_send()
-        if q < DIRECT:
-            half_plus(q).wait_send()
-            half_minus(q).wait_send()
-        else:
-            y_two(q).wait_send()
 
     for dx in range(4):
         s_copy(dx).wait_send()

time: 83.8 us -> 80.8 us (0.964)
  Pallas kernels: 83 us -> 80 us
    pallas_call x1, Pallas kernels: 83 us -> 80 us  [local(): pl.pallas_call(kernel, out_shape=pltpu.VMEM((256, 128), F32), in_specs=[h...]
where the time goes in v5:
time: 80.8 us; the launch traced here: 80.6 us
  Pallas kernels  80 us (99%)
    pallas_call x1, Pallas kernels, local(): pl.pallas_call(kernel, out_shape=pltpu.VMEM((256, 128), F32), in_specs=[h...  80 us

profile of v5, /device:TPU:1, one launch (start us, length us, event | category | flops | bytes accessed | tf_op | source)
XLA Modules:
  0.0 80.6 jit_solution(17689973762720878303)
XLA Ops:
  0.0 80.0 %shard_map.73 = f32[256,128]{1,0:T(8,128)S(1)} custom-call(bf16[16,512]{1,0:T(8,128)(2,1)} %bitcast.13, bf16[8192,128]{1,0:T(8,128)(2,1)} %bitcast.12, bf16[16384,64]{1,0:T(8,128)(2,1)} %bitcast.11, s32[2,512]{1,0:T(2,128)} %bitcast.14, f32[1,128]{1,0:T(1,128)} %bitcast.15, f32[1,64]{1,0:T(1,128)} %bitcast.16, f32[1,128]{1,0:T(1,128)} %bitcast.17), custom_call_target="tpu_custom_call" | custom-call | tf_op jit(solution)/shard_map/pallas_call | solution.py:399
  80.0 0.7 copy.9
